TPU v7x, 32 devices: a whole 2x2x4 slice. The times are simulated.
32 devices in a mesh: seq: 8 (over z, x), head: 4 (over y, core).
Axes of the slice: x: 2, y: 2, z: 4, core: 2. Of those that a mesh axis runs over, the one named last changes fastest.
Arguments:
- tokens: bfloat16 [4096, 2048], P('seq'), may hold values from -6 to 6
- cotangent: bfloat16 [4096, 2048], P('seq'), may hold values from -6 to 6
- w_query: bfloat16 [2048, 2048], P(None, 'head'), may hold values from -0.61871843 to 0.61871843
- w_key: bfloat16 [2048, 2048], P(None, 'head'), may hold values from -0.61871843 to 0.61871843
- w_value: bfloat16 [2048, 2048], P(None, 'head'), may hold values from -0.61871843 to 0.61871843
- w_out: bfloat16 [2048, 2048], P('head'), may hold values from -0.61871843 to 0.61871843
- seeds: int32 [4], replicated, may hold values from 0 to 32748
Outputs:
- attended: bfloat16 [4096, 2048], P('seq', 'head')
- grad_tokens: bfloat16 [4096, 2048], P('seq', 'head')
- grad_w_query: float32 [2048, 2048], P('seq', 'head')
- grad_w_key: float32 [2048, 2048], P('seq', 'head')
- grad_w_value: float32 [2048, 2048], P('seq', 'head')
- grad_w_out: float32 [2048, 2048], P('head', 'seq')
All inputs are finite; a program needn't handle non-finite values.
Results may differ from a plain program's by a relative error of at most 0.013.
The roundings to bfloat16 on the way count: a program that leaves them out, or rounds other values in their place, can miss the bound.
Values may be sent and summed in bfloat16 or wider, within the bound.
A program may use at most 192 MiB of HBM per device.

v0:
```python
import math

import jax
import jax.numpy as jnp
from jax import lax
from jax.sharding import PartitionSpec as P

DH = 128
LEAF = 128


soft_cap = 6.0
noise_level = 0.5
prime_mod = 32749


def swapped(shard, axis, apart):
    return lax.ppermute(shard, axis, [(i, i ^ 1 << apart) for i in range(lax.axis_size(axis))])


def noise_grid(row_ids, col_ids, seed_value):
    row_part = row_ids[:, None]
    col_part = col_ids[None, :]
    hashed = (
        row_part * 7919 % prime_mod + col_part * 10007 % prime_mod + seed_value * 31337 % prime_mod
    ) % prime_mod
    hashed = (hashed * hashed + col_part) % prime_mod
    hashed = (hashed * hashed + row_part) % prime_mod
    return hashed.astype(jnp.float32) * (2.0 / (prime_mod - 1)) - 1.0


def perturb(weight, noise, axis_no):
    as_float = weight.astype(jnp.float32)
    spread = jnp.sqrt(jnp.mean(as_float * as_float, axis=axis_no, keepdims=True) + 1e-06)
    return (as_float + noise_level * spread * noise).astype(jnp.bfloat16)


def halve_rows(rows_in):
    paired = rows_in.astype(jnp.float32).reshape((rows_in.shape[0] // 2, 2) + rows_in.shape[1:])
    return ((paired[:, 0] + paired[:, 1]) * 0.5).astype(jnp.bfloat16)


def expand_rows(grad_rows):
    return jnp.repeat(grad_rows * 0.5, 2, axis=0)


def flip_pairs(blocks):
    return blocks.reshape((blocks.shape[0] // 2, 2) + blocks.shape[1:])[:, ::-1].reshape(
        blocks.shape
    )


def group_view(array_in, groups):
    return array_in.reshape((groups, array_in.shape[0] // groups) + array_in.shape[1:])


def forward_set(queries, key_rows, value_rows, multiplicity):
    scale_q = 1.0 / math.sqrt(queries.shape[-1])
    scores = (
        jnp.einsum("gqhd,gkhd->gqhk", queries, key_rows, preferred_element_type=jnp.float32)
        * scale_q
    )
    capped = jnp.tanh(scores / soft_cap)
    weights = multiplicity * jnp.exp(soft_cap * capped)
    numerator = jnp.einsum(
        "gqhk,gkhd->gqhd",
        weights.astype(jnp.bfloat16),
        value_rows,
        preferred_element_type=jnp.float32,
    )
    return (jnp.sum(weights, axis=-1), numerator)


def backward_set(queries, key_rows, value_rows, grad_out, weight_sum, row_delta, multiplicity):
    scale_q = 1.0 / math.sqrt(queries.shape[-1])
    scores = (
        jnp.einsum("gqhd,gkhd->gqhk", queries, key_rows, preferred_element_type=jnp.float32)
        * scale_q
    )
    capped = jnp.tanh(scores / soft_cap)
    weights = multiplicity * jnp.exp(soft_cap * capped)
    probability = weights / weight_sum[..., None]
    grad_values = jnp.einsum(
        "gqhk,gqhd->gkhd",
        probability.astype(jnp.bfloat16),
        grad_out,
        preferred_element_type=jnp.float32,
    )
    grad_prob = jnp.einsum(
        "gqhd,gkhd->gqhk", grad_out, value_rows, preferred_element_type=jnp.float32
    )
    grad_scores = (
        probability * (grad_prob - row_delta[..., None]) * (1.0 - capped * capped)
    ).astype(jnp.bfloat16)
    grad_queries = (
        jnp.einsum("gqhk,gkhd->gqhd", grad_scores, key_rows, preferred_element_type=jnp.float32)
        * scale_q
    )
    grad_keys = (
        jnp.einsum("gqhk,gqhd->gkhd", grad_scores, queries, preferred_element_type=jnp.float32)
        * scale_q
    )
    return (grad_queries, grad_keys, grad_values)


def arrange(queries, key_rows, value_rows, flipped):
    groups = key_rows.shape[0] // LEAF
    key_view = group_view(key_rows, groups)
    value_view = group_view(value_rows, groups)
    if flipped:
        key_view = flip_pairs(key_view)
        value_view = flip_pairs(value_view)
    return (group_view(queries, groups), key_view, value_view, groups)


def lower_side(seq_idx, bit_no):
    return seq_idx // 2**bit_no % 2 == 0


def swap_levels(pair_rows, levels_used, seq_idx):
    partners = []
    for bit_no in range(levels_used):
        other_rows = swapped(pair_rows, "seq", bit_no)
        partners.append(other_rows)
        if bit_no + 1 < levels_used:
            mine_half = halve_rows(pair_rows)
            other_half = halve_rows(other_rows)
            pair_rows = jnp.where(
                lower_side(seq_idx, bit_no),
                jnp.concatenate([mine_half, other_half], axis=0),
                jnp.concatenate([other_half, mine_half], axis=0),
            )
    return partners


def return_swaps(grads, seq_idx):
    upper_grad = None
    for bit_no in reversed(range(len(grads))):
        send_rows = grads[bit_no]
        own_part = jnp.zeros_like(send_rows)
        if upper_grad is not None:
            wide_rows = expand_rows(upper_grad)
            half_rows = wide_rows.shape[0] // 2
            first_rows = wide_rows[:half_rows]
            second_rows = wide_rows[half_rows:]
            lower = lower_side(seq_idx, bit_no)
            own_part = jnp.where(lower, first_rows, second_rows)
            send_rows = send_rows + jnp.where(lower, second_rows, first_rows)
        back_rows = swapped(send_rows, "seq", bit_no)
        upper_grad = own_part + back_rows
    return upper_grad


def body(tokens, cotangent, w_query, w_key, w_value, w_out, seeds):
    seq_count = lax.axis_size("seq")
    seq_bits = seq_count.bit_length() - 1
    seq_idx = lax.axis_index("seq")
    head_idx = lax.axis_index("head")
    tok_rows = tokens.shape[0]
    model_width = tokens.shape[1]
    head_cols = w_query.shape[1]
    local_heads = head_cols // DH
    local_bits = (tok_rows // LEAF).bit_length() - 1
    all_ids = jnp.arange(model_width, dtype=jnp.int32)
    own_ids = head_idx * head_cols + jnp.arange(head_cols, dtype=jnp.int32)
    query_w = perturb(w_query, noise_grid(all_ids, own_ids, seeds[0]), 0)
    key_w = perturb(w_key, noise_grid(all_ids, own_ids, seeds[1]), 0)
    value_w = perturb(w_value, noise_grid(all_ids, own_ids, seeds[2]), 0)
    out_w = perturb(w_out, noise_grid(own_ids, all_ids, seeds[3]), 1)
    head_shape = (tok_rows, local_heads, DH)
    queries = (
        jnp.dot(tokens, query_w, preferred_element_type=jnp.float32)
        .astype(jnp.bfloat16)
        .reshape(head_shape)
    )
    key_all = (
        jnp.dot(tokens, key_w, preferred_element_type=jnp.float32)
        .astype(jnp.bfloat16)
        .reshape(head_shape)
    )
    value_all = (
        jnp.dot(tokens, value_w, preferred_element_type=jnp.float32)
        .astype(jnp.bfloat16)
        .reshape(head_shape)
    )
    key_levels = [key_all]
    value_levels = [value_all]
    for level_no in range(local_bits):
        key_levels.append(halve_rows(key_levels[-1]))
        value_levels.append(halve_rows(value_levels[-1]))
    own_pair = jnp.stack([key_levels[local_bits], value_levels[local_bits]], axis=1)
    partners = swap_levels(own_pair, seq_bits, seq_idx)
    all_sets = [(key_levels[0], value_levels[0], False, 1.0)]
    all_sets = all_sets + [
        (key_levels[level_no], value_levels[level_no], True, 2.0**level_no)
        for level_no in range(local_bits)
    ]
    all_sets = all_sets + [
        (pair_rows[:, 0], pair_rows[:, 1], False, 2.0 ** (local_bits + bit_no))
        for bit_no, pair_rows in enumerate(partners)
    ]
    weight_sum = jnp.zeros((tok_rows, local_heads), jnp.float32)
    numerator = jnp.zeros(head_shape, jnp.float32)
    for key_rows, value_rows, flipped, multiplicity in all_sets:
        query_view, key_view, value_view, groups = arrange(queries, key_rows, value_rows, flipped)
        part_sum, part_num = forward_set(query_view, key_view, value_view, multiplicity)
        weight_sum = weight_sum + part_sum.reshape(tok_rows, local_heads)
        numerator = numerator + part_num.reshape(head_shape)
    attention = (numerator / weight_sum[..., None]).astype(jnp.bfloat16)
    flat_attention = attention.reshape(tok_rows, head_cols)
    out_terms_all = jnp.dot(flat_attention, out_w, preferred_element_type=jnp.float32)
    attended = lax.psum_scatter(out_terms_all, "head", scatter_dimension=1, tiled=True).astype(
        jnp.bfloat16
    )
    grad_attention = jnp.dot(cotangent, out_w.T, preferred_element_type=jnp.float32).astype(
        jnp.bfloat16
    )
    grad_heads = grad_attention.reshape(head_shape)
    row_delta = jnp.sum(grad_heads.astype(jnp.float32) * attention.astype(jnp.float32), axis=-1)
    grad_q = jnp.zeros(head_shape, jnp.float32)
    set_grads = []
    for key_rows, value_rows, flipped, multiplicity in all_sets:
        query_view, key_view, value_view, groups = arrange(queries, key_rows, value_rows, flipped)
        dq_part, dk_part, dv_part = backward_set(
            query_view,
            key_view,
            value_view,
            group_view(grad_heads, groups),
            group_view(weight_sum, groups),
            group_view(row_delta, groups),
            multiplicity,
        )
        grad_q = grad_q + dq_part.reshape(head_shape)
        if flipped:
            dk_part = flip_pairs(dk_part)
            dv_part = flip_pairs(dv_part)
        set_grads.append(
            jnp.stack([dk_part.reshape(key_rows.shape), dv_part.reshape(value_rows.shape)], axis=1)
        )
    cross_grads = set_grads[1 + local_bits :]
    upper_grad = return_swaps(cross_grads, seq_idx)
    for level_no in reversed(range(local_bits)):
        upper_grad = set_grads[level_no + 1] + expand_rows(upper_grad)
    upper_grad = upper_grad + set_grads[0]
    dq_flat = grad_q.astype(jnp.bfloat16).reshape(tok_rows, head_cols)
    dk_flat = upper_grad[:, 0].astype(jnp.bfloat16).reshape(tok_rows, head_cols)
    dv_flat = upper_grad[:, 1].astype(jnp.bfloat16).reshape(tok_rows, head_cols)
    input_terms = jnp.dot(dq_flat, query_w.T, preferred_element_type=jnp.float32)
    input_terms = input_terms + jnp.dot(dk_flat, key_w.T, preferred_element_type=jnp.float32)
    input_terms = input_terms + jnp.dot(dv_flat, value_w.T, preferred_element_type=jnp.float32)
    grad_tokens = lax.psum_scatter(input_terms, "head", scatter_dimension=1, tiled=True).astype(
        jnp.bfloat16
    )
    grads_cat = jnp.concatenate([dq_flat, dk_flat, dv_flat], axis=1)
    both_shares = lax.psum_scatter(
        jnp.concatenate(
            [
                lax.dot_general(
                    tokens, grads_cat, (((0,), (0,)), ((), ())), preferred_element_type=jnp.float32
                ),
                lax.dot_general(
                    cotangent,
                    flat_attention,
                    (((0,), (0,)), ((), ())),
                    preferred_element_type=jnp.float32,
                ),
            ],
            axis=1,
        ),
        "seq",
        scatter_dimension=0,
        tiled=True,
    )
    in_share = both_shares[:, : 3 * head_cols]
    out_share = both_shares[:, 3 * head_cols :]
    grad_w_query = in_share[:, :head_cols]
    grad_w_key = in_share[:, head_cols : 2 * head_cols]
    grad_w_value = in_share[:, 2 * head_cols :]
    return (attended, grad_tokens, grad_w_query, grad_w_key, grad_w_value, out_share.T)


def solution(mesh):
    in_specs = (
        P("seq", None),
        P("seq", None),
        P(None, "head"),
        P(None, "head"),
        P(None, "head"),
        P("head", None),
        P(),
    )
    out_specs = (
        P("seq", "head"),
        P("seq", "head"),
        P("seq", "head"),
        P("seq", "head"),
        P("seq", "head"),
        P("head", "seq"),
    )
    return jax.shard_map(body, mesh=mesh, in_specs=in_specs, out_specs=out_specs, check_vma=False)
```

profile of v0, /device:TPU:0, one launch (start us, length us, event | category | flops | bytes accessed | tf_op | source)
XLA Modules:
  0.0 689.4 jit_solution(9782048533832664069)
XLA Ops:
  16.1 11.2 %fusion.108 = bf16[512,512]{0,1:T(8,128)(2,1)S(1)} fusion(bf16[512,2048]{1,0:T(8,128)(2,1)S(1)} %copy-done, bf16[2048,512]{1,0:T(8,128)(2,1)} %param.11, s32[512]{0:T(512)S(1)} %iota_add_fusion, s32[]{:T(128)S(6)} %select_n.198, s32[512]{0:T(512)S(1)} %get-tuple-element.71, s32[2048]{0:T(1024)S(1)} %add_select_fusion.13, f32[512]{0:T(512)S(1)} %sqrt_multiply_fusion.3), kind=kOutput, calls=%fused_computation.163 | convolution fusion | flops 1106509824 | bytes 4732932 | tf_op jit(solution)/shard_map/dot_general | solution.py:182
  28.5 2.8 reshape.706
  33.8 21.4 %fusion.3 = (bf16[2048,512]{1,0:T(8,128)(2,1)S(1)}, bf16[2048,512]{1,0:T(8,128)(2,1)}) fusion(bf16[2048,512]{1,0:T(8,128)(2,1)} %param.10, s32[]{:T(128)S(6)} %select_n.202, f32[512]{0:T(512)S(1)} %get-tuple-element.73, s32[512]{0:T(512)S(1)} %iota_add_fusion, s32[512]{0:T(512)S(1)} %get-tuple-element.71, s32[2048]{0:T(1024)S(1)} %add_select_fusion.13, ...), kind=kLoop, calls=%fused_computation.28 | loop fusion | flops 63963136 | bytes 8405000 | tf_op jit(solution)/shard_map/convert_element_type | solution.py:35
  59.2 2.6 reshape.707
  65.7 2.9 collective-permute-start
  72.0 2.9 convolution_convert_fusion.1
  80.4 5.7 rev.24
  92.5 5.6 rev.25
  105.2 11.4 %fusion.7 = bf16[512,2048]{1,0:T(8,128)(2,1)S(1)} fusion(bf16[512,2048]{1,0:T(8,128)(2,1)} %param.12, s32[512]{0:T(512)S(1)} %copy-done.61, s32[]{:T(128)S(6)} %select_n.219, s32[2048]{0:T(1024)S(1)} %add_select_fusion.12, s32[512]{0:T(512)S(1)} %copy-done.64, f32[512]{0:T(512)S(1)} %copy-done.65), kind=kLoop, calls=%fused_computation.32 | loop fusion | flops 32505856 | bytes 4208644 | tf_op jit(solution)/shard_map/convert_element_type | solution.py:35
  135.0 2.9 copy.200
  137.9 2.6 copy.242
  153.3 2.6 copy.219
  158.7 2.7 collective-permute-start.2
  168.5 4.3 collective-permute-done.2
  174.2 4.1 multiply_reduce_fusion
  184.7 2.6 copy.235
  223.1 3.7 fusion.124
  227.6 3.3 fusion.240
  244.9 14.3 %collective-permute-done.3 = f32[128,2,4,128]{0,3,2,1:T(8,128)S(1)} collective-permute-done((f32[128,2,4,128]{0,3,2,1:T(8,128)S(1)}, f32[128,2,4,128]{0,3,2,1:T(8,128)S(1)}, u32[]{:S(2)}, u32[]{:S(2)}) %collective-permute-start.3) | collective-permute-done | bytes 524320 | tf_op jit(solution)/shard_map/ppermute | solution.py:18
  268.6 3.9 fusion.116
  273.9 6.9 collective-permute-done.4
  294.5 2.6 copy.270
  303.3 2.6 copy.294
  305.9 2.6 copy.267
  310.8 5.0 fusion.241
  332.3 12.1 %add_add_fusion.3 = f32[512,2048]{1,0:T(8,128)} fusion(f32[512,2048]{1,0:T(8,128)S(1)} %copy-done.1, f32[512,2048]{1,0:T(8,128)S(1)} %fusion.228, bf16[64,8,4,128]{3,2,1,0:T(4,128)(2,1)S(1)} %bitcast.603, bf16[2048,512]{1,0:T(8,128)(2,1)S(1)} %copy-done.24, s32[512]{0:T(512)S(1)} %copy-done.61, s32[]{:T(128)S(6)} %select_n.198, s32[512]{0:T(512)S(1)} %copy-done.63, ...), kind=kOutput, calls=%fused_computation.82 | convolution fusion | flops 1108344832 | bytes 15218692 | tf_op jit(solution)/shard_map/dot_general | solution.py:250
  345.5 3.0 convolution_bitcast_fusion.1
  348.7 3.5 convolution_bitcast_fusion
  352.2 6.5 pad_maximum_fusion
  360.8 28.3 %reduce-scatter.6.cloned.1.call-done = f32[512,512]{1,0:T(8,128)} async-done(((f32[512,2048]{1,0:T(8,128)}), f32[512,512]{1,0:T(8,128)}) %reduce-scatter.6.cloned.1.call-update) | async-done | bytes 1048592 | tf_op jit(solution)/shard_map/reduce_scatter | solution.py:251
  391.2 284.6 %reduce-scatter.8.cloned.1.call-done = f32[256,2048]{0,1:T(8,128)} async-done(((f32[2048,2048]{0,1:T(8,128)}), f32[256,2048]{0,1:T(8,128)}) %reduce-scatter.8.cloned.1.call-update) | async-done | bytes 2097168 | tf_op jit(solution)/shard_map/reduce_scatter | solution.py:255
  675.8 2.7 slice_bitcast_fusion
  (293 shorter events, 198.0 us)
Async XLA Ops:
  7.2 8.9 %copy-start = (bf16[512,2048]{1,0:T(8,128)(2,1)S(1)}, bf16[512,2048]{1,0:T(8,128)(2,1)}, u32[]{:S(2)}) copy-start(bf16[512,2048]{1,0:T(8,128)(2,1)} %param.7) | copy-start | bytes 6291460
  7.2 351.5 %reduce-scatter.4.cloned.1.call-start = ((), (), s32[]{:S(2)}) async-start(), calls=%async_computation.3 | async-start | bytes 5242880 | tf_op jit(solution)/shard_map/reduce_scatter | solution.py:212
  10.7 4.9 copy-start.23
  10.7 23.1 %copy-start.60 = (s32[512]{0:T(512)}, s32[512]{0:T(512)S(1)}, u32[]{:S(2)}) copy-start(s32[512]{0:T(512)S(1)} %iota_add_fusion) | copy-start | bytes 6148
  11.3 22.6 %copy-start.62 = (s32[512]{0:T(512)}, s32[512]{0:T(512)S(1)}, u32[]{:S(2)}) copy-start(s32[512]{0:T(512)S(1)} %get-tuple-element.71) | copy-start | bytes 6148
  16.1 11.2 %copy-start.66 = (f32[512]{0:T(512)}, f32[512]{0:T(512)S(1)}, u32[]{:S(2)}) copy-start(f32[512]{0:T(512)S(1)} %sqrt_multiply_fusion.3) | copy-start | bytes 6148
  65.7 78.4 %collective-permute-start = (bf16[128,2,4,128]{3,0,2,1:T(8,128)(2,1)}, bf16[128,2,4,128]{3,0,2,1:T(8,128)(2,1)}, u32[]{:S(2)}, u32[]{:S(2)}) collective-permute-start(bf16[128,2,4,128]{3,0,2,1:T(8,128)(2,1)} %pad_maximum_fusion.2), channel_id=1, source_target_pairs={{0,4},{4,0},{8,12},{12,8},{16,20},{20,16},{24,28},{28,24},{1,5},{5... | collective-permute-start | bytes 786440 | tf_op jit(solution)/shard_map/ppermute | solution.py:18
  77.7 23.6 %copy-start.6 = (bf16[4,128,4,128]{1,0,3,2:T(4,128)(2,1)S(1)}, bf16[4,128,4,128]{1,0,3,2:T(4,128)(2,1)}, u32[]{:S(2)}) copy-start(bf16[4,128,4,128]{1,0,3,2:T(4,128)(2,1)} %reshape_reshape.14) | copy-start | bytes 1572868
  100.5 18.3 %copy-start.41 = (bf16[2,128,4,128]{3,1,0,2:T(8,128)(2,1)}, bf16[2,128,4,128]{3,1,0,2:T(8,128)(2,1)S(1)}, u32[]{:S(2)}) copy-start(bf16[2,128,4,128]{3,1,0,2:T(8,128)(2,1)S(1)} %reverse_bitcast_fusion) | copy-start | bytes 786436
  101.2 4.0 copy-start.61
  101.2 4.0 copy-start.64
  101.2 4.0 copy-start.65
  105.2 11.4 %copy-start.25 = (bf16[512,2048]{1,0:T(8,128)(2,1)S(1)}, bf16[512,2048]{1,0:T(8,128)(2,1)}, u32[]{:S(2)}) copy-start(bf16[512,2048]{1,0:T(8,128)(2,1)} %param.8) | copy-start | bytes 6291460
  145.7 11.2 %collective-permute-start.1 = (bf16[128,2,4,128]{3,0,2,1:T(8,128)(2,1)S(1)}, bf16[128,2,4,128]{3,0,2,1:T(8,128)(2,1)}, u32[]{:S(2)}, u32[]{:S(2)}) collective-permute-start(bf16[128,2,4,128]{3,0,2,1:T(8,128)(2,1)S(1)} %maximum_select_fusion), channel_id=1, source_target_pairs={{0,8},{4,12},{8,0},{12,4},{16,24},{20,28},{24,16},{28,20},{1,9},{5... | collective-permute-start | bytes 786440 | tf_op jit(solution)/shard_map/ppermute | solution.py:18
  158.7 14.1 %collective-permute-start.2 = (bf16[128,2,4,128]{3,0,2,1:T(8,128)(2,1)S(1)}, bf16[128,2,4,128]{3,0,2,1:T(8,128)(2,1)}, u32[]{:S(2)}, u32[]{:S(2)}) collective-permute-start(bf16[128,2,4,128]{3,0,2,1:T(8,128)(2,1)S(1)} %maximum_select_fusion.1), channel_id=1, source_target_pairs={{0,16},{4,20},{8,24},{12,28},{16,0},{20,4},{24,8},{28,12},{1,17},{... | collective-permute-start | bytes 786440 | tf_op jit(solution)/shard_map/ppermute | solution.py:18
  168.5 9.8 %copy-start.20 = (bf16[2,2,128,4,128]{4,2,3,1,0:T(8,128)(2,1)S(1)}, bf16[2,2,128,4,128]{4,2,3,1,0:T(8,128)(2,1)}, u32[]{:S(2)}) copy-start(bf16[2,2,128,4,128]{4,2,3,1,0:T(8,128)(2,1)} %copy.195) | copy-start | bytes 1572868
  168.5 9.8 %copy-start.37 = (f32[4,4,128,128]{3,2,1,0:T(8,128)S(1)}, f32[4,4,128,128]{3,2,1,0:T(8,128)}, u32[]{:S(2)}) copy-start(f32[4,4,128,128]{3,2,1,0:T(8,128)} %get-tuple-element.67) | copy-start | bytes 3145732
  168.5 9.8 %copy-start.55 = (bf16[4,128,4,128]{1,0,3,2:T(4,128)(2,1)S(1)}, bf16[4,128,4,128]{1,0,3,2:T(4,128)(2,1)}, u32[]{:S(2)}) copy-start(bf16[4,128,4,128]{1,0,3,2:T(4,128)(2,1)} %reshape_reshape.16) | copy-start | bytes 1572868
  174.1 5.5 copy-start.54
  180.9 6.3 copy-start.40
  223.1 4.5 copy-start.3
  230.8 158.3 %reduce-scatter.6.cloned.1.call-start = ((), (), s32[]{:S(2)}) async-start(), calls=%async_computation.4 | async-start | bytes 5242880 | tf_op jit(solution)/shard_map/reduce_scatter | solution.py:251
  230.9 4.5 copy-start.34
  232.3 4.6 copy-start.7
  232.3 4.6 copy-start.49
  234.3 3.7 copy-start.51
  234.3 24.9 %collective-permute-start.3 = (f32[128,2,4,128]{0,3,2,1:T(8,128)S(1)}, f32[128,2,4,128]{0,3,2,1:T(8,128)S(1)}, u32[]{:S(2)}, u32[]{:S(2)}) collective-permute-start(f32[128,2,4,128]{0,3,2,1:T(8,128)S(1)} %pad_maximum_fusion.1), channel_id=1, source_target_pairs={{0,16},{4,20},{8,24},{12,28},{16,0},{20,4},{24,8},{28,12},{1,17},{... | collective-permute-start | bytes 1572872 | tf_op jit(solution)/shard_map/ppermute | solution.py:18
  266.6 14.2 %collective-permute-start.4 = (f32[128,2,4,128]{0,3,2,1:T(8,128)}, f32[128,2,4,128]{0,3,2,1:T(8,128)}, u32[]{:S(2)}, u32[]{:S(2)}) collective-permute-start(f32[128,2,4,128]{0,3,2,1:T(8,128)} %maximum_add_fusion.2), channel_id=1, source_target_pairs={{0,8},{4,12},{8,0},{12,4},{16,24},{20,28},{24,16},{28,20},{1,9},{5... | collective-permute-start | bytes 1572872 | tf_op jit(solution)/shard_map/ppermute | solution.py:18
  273.9 16.1 %copy-start.16 = (bf16[2,256,4,128]{1,3,2,0:T(8,128)(2,1)S(1)}, bf16[2,256,4,128]{1,3,2,0:T(8,128)(2,1)}, u32[]{:S(2)}) copy-start(bf16[2,256,4,128]{1,3,2,0:T(8,128)(2,1)} %copy-done.15) | copy-start | bytes 1572868
  273.9 16.1 %copy-start.18 = (bf16[2,256,4,128]{1,0,3,2:T(2,128)(2,1)S(1)}, bf16[2,256,4,128]{1,0,3,2:T(2,128)(2,1)}, u32[]{:S(2)}) copy-start(bf16[2,256,4,128]{1,0,3,2:T(2,128)(2,1)} %reshape_reshape.15) | copy-start | bytes 1572868
  289.5 30.6 %collective-permute-start.5 = (f32[128,2,4,128]{0,3,2,1:T(8,128)}, f32[128,2,4,128]{0,3,2,1:T(8,128)}, u32[]{:S(2)}, u32[]{:S(2)}) collective-permute-start(f32[128,2,4,128]{0,3,2,1:T(8,128)} %maximum_add_fusion.3), channel_id=1, source_target_pairs={{0,4},{4,0},{8,12},{12,8},{16,20},{20,16},{24,28},{28,24},{1,5},{5... | collective-permute-start | bytes 1572872 | tf_op jit(solution)/shard_map/ppermute | solution.py:18
  344.5 331.3 %reduce-scatter.8.cloned.1.call-start = ((), (), s32[]{:S(2)}) async-start(), calls=%async_computation.5 | async-start | bytes 18874368 | tf_op jit(solution)/shard_map/reduce_scatter | solution.py:255
  (45 other events, 98.4 us)
Sparse Core Ops, SparseCore 0:
  231.0 43.8 reduce-scatter.3
  344.6 44.4 reduce-scatter.5
  392.9 282.8 reduce-scatter.7
where the time goes:
time: 702 us; the launch traced here: 689 us
  waiting for transfers between devices  339 us (48%)
  local copies, waits for them, and re-layouts  143 us (20%)
  matrix products  105 us (15%)
  other arithmetic  76.6 us (11%)
  between operations  17.7 us (3%)
  starting transfers between devices  7.93 us (1%)
    reduce_scatter x1, waiting for transfers between devices, body(): lax.psum_scatter(jnp.concatenate([lax.dot_general(tokens, grads_cat, (((0...  285 us
    convert_element_type x2, other arithmetic, perturb(): return (as_float + noise_level * spread * noise).astype(jnp.bfloat16)  32.8 us
    reduce_scatter x1, waiting for transfers between devices, body(): lax.psum_scatter(input_terms, 'head', scatter_dimension=1, tiled=True)  28.3 us
    ppermute x6, waiting for transfers between devices, swapped(): lax.ppermute(shard, axis, [(i, i ^ 1 << apart) for i in range(lax.axis_si...  25.5 us
    rev x5, local copies, waits for them, and re-layouts, flip_pairs(): blocks.reshape((blocks.shape[0] // 2, 2) + blocks.shape[1:])[:, ::-1]  18 us
    unnamed x141, local copies, waits for them, and re-layouts  16.1 us
  transfers between devices with their start and end apart: 9, of which 5 were waited for; matrix products, arithmetic and copies ran while one was open for 28% of the time, Pallas kernels for 0%

commit v1 on v0

v1 whole, which is shorter than its diff:
```python
import functools
import math

import jax
import jax.numpy as jnp
import numpy as np
from jax import lax
from jax.experimental import pallas as pl
from jax.experimental.pallas import tpu as pltpu
from jax.sharding import PartitionSpec as P

DH = 128
LEAF = 128
LANES = 128

soft_cap = 6.0
noise_level = 0.5
prime_mod = 32749
inv_prime = 1.0 / prime_mod
BF = jnp.bfloat16
F32 = jnp.float32


def centre(residue):
    return jnp.where(residue > prime_mod // 2, residue - prime_mod, residue)


def dot32(left, right):
    return jnp.dot(left, right, preferred_element_type=F32)


def dot_rows(left, right):
    return lax.dot_general(left, right, (((0,), (0,)), ((), ())), preferred_element_type=F32)


def perturb_kernel(axis_no, row_hash, row_id, col_hash, col_id, w_ref, out_ref):
    rows, cols = w_ref.shape
    chunk = min(rows, 256)
    if axis_no == 0:

        def add_squares(i, total):
            part = w_ref[pl.ds(pl.multiple_of(i * chunk, chunk), chunk), :].astype(F32)
            return total + jnp.sum(part * part, axis=0, keepdims=True)

        squares = lax.fori_loop(0, rows // chunk, add_squares, jnp.zeros((1, cols), F32))
        spread = noise_level * jnp.sqrt(squares * (1.0 / rows) + 1e-06)
    else:
        whole = w_ref[...].astype(F32)
        spread = noise_level * jnp.sqrt(
            jnp.sum(whole * whole, axis=1, keepdims=True) * (1.0 / cols) + 1e-06
        )
    step_u = spread * (2.0 / (prime_mod - 1))

    def do_rows(i, carry):
        here = pl.ds(pl.multiple_of(i * chunk, chunk), chunk)
        r_hash = row_hash[here, :]
        r_id = row_id[here, :]
        for j in range(cols // LANES):
            at = slice(j * LANES, (j + 1) * LANES)
            h = r_hash + col_hash[:, at]
            x = h * h + col_id[:, at]
            h = x - (x.astype(F32) * inv_prime).astype(jnp.int32) * prime_mod
            x = h * h + r_id
            h = x - (x.astype(F32) * inv_prime - 0.0078125).astype(jnp.int32) * prime_mod
            h = jnp.where(h >= prime_mod, h - prime_mod, h)
            if axis_no == 0:
                slope, base = step_u[:, at], spread[:, at]
            else:
                slope, base = step_u, spread
            out_ref[here, at] = (
                w_ref[here, at].astype(F32) + (h.astype(F32) * slope - base)
            ).astype(BF)
        return carry

    lax.fori_loop(0, rows // chunk, do_rows, 0)


def perturb(weight, row_hash, row_id, col_hash, col_id, axis_no):
    rows, cols = weight.shape
    if axis_no == 0:
        block = (rows, min(cols, 128))
        row_map, col_map, w_map = (lambda i: (0, 0)), (lambda i: (0, i)), (lambda i: (0, i))
        steps = cols // block[1]
    else:
        block = (min(rows, 128), cols)
        row_map, col_map, w_map = (lambda i: (i, 0)), (lambda i: (0, 0)), (lambda i: (i, 0))
        steps = rows // block[0]
    row_spec = pl.BlockSpec((block[0], LANES), row_map)
    col_spec = pl.BlockSpec((1, block[1]), col_map)
    return pl.pallas_call(
        functools.partial(perturb_kernel, axis_no),
        grid=(steps,),
        in_specs=[row_spec, row_spec, col_spec, col_spec, pl.BlockSpec(block, w_map)],
        out_specs=pl.BlockSpec(block, w_map),
        out_shape=jax.ShapeDtypeStruct((rows, cols), BF),
        compiler_params=pltpu.CompilerParams(vmem_limit_bytes=40 << 20),
        cost_estimate=pl.CostEstimate(
            flops=30 * rows * cols, bytes_accessed=4 * rows * cols, transcendentals=0
        ),
        name="perturb",
    )(row_hash, row_id, col_hash, col_id, weight)


def pair_mean(count):
    r = lax.broadcasted_iota(jnp.int32, (count // 2, count), 0)
    c = lax.broadcasted_iota(jnp.int32, (count // 2, count), 1)
    return jnp.where(c // 2 == r, 0.5, 0.0).astype(BF)


def coarse_kernel(k_ref, v_ref, *outs):
    cols = k_ref.shape[1]
    for n, src in enumerate((k_ref, v_ref)):
        rows = src[...]
        for out in outs:
            count = rows.shape[0]
            if count >= 16:
                rows = dot32(pair_mean(count), rows).astype(BF)
            out[:, n * cols : (n + 1) * cols] = rows


def attention_kernel(
    tok_rows,
    cross_rows,
    q_ref,
    k_ref,
    v_ref,
    do_ref,
    k1_ref,
    v1_ref,
    kx_ref,
    vx_ref,
    att_ref,
    dq_ref,
    dk_ref,
    dv_ref,
    dkx_ref,
    dvx_ref,
):
    pair = 2 * LEAF
    groups = tok_rows // pair
    scale_q = 1.0 / math.sqrt(DH)
    total_keys = pair + LEAF + cross_rows
    rows = lax.broadcasted_iota(jnp.int32, (total_keys, 1), 0)
    log_m = jnp.where(rows < pair, 0, (rows - pair) // LEAF + 1).astype(F32)
    dk1 = [None] * groups
    dv1 = [None] * groups
    dkx = None
    dvx = None
    for g in range(groups):
        own = slice(g * pair, (g + 1) * pair)
        other = slice((g ^ 1) * LEAF, ((g ^ 1) + 1) * LEAF)
        keys = jnp.concatenate([k_ref[own, :], k1_ref[other, :], kx_ref[...]], axis=0)
        values = jnp.concatenate([v_ref[own, :], v1_ref[other, :], vx_ref[...]], axis=0)
        q = q_ref[own, :]
        do = do_ref[own, :]
        do_t = do.astype(F32).T
        s = dot32(keys, q.astype(F32).T.astype(BF))
        t = jnp.tanh(s * (scale_q / soft_cap))
        w = jnp.exp2(t * (soft_cap * math.log2(math.e)) + log_m)
        weight_sum = jnp.sum(w, axis=0, keepdims=True)
        values_t = values.astype(F32).T.astype(BF)
        att_t = (dot32(values_t, w.astype(BF)) / weight_sum).astype(BF).astype(F32)
        att_ref[own, :] = att_t.T.astype(BF)
        delta = jnp.sum(att_t * do_t, axis=0, keepdims=True)
        p = w * (1.0 / weight_sum)
        dv = dot32(p.astype(BF), do)
        dp = dot32(values, do_t.astype(BF))
        grad = (p * (dp - delta) * (1.0 - t * t)).astype(BF)
        dk = dot32(grad, q) * scale_q
        keys_t = keys.astype(F32).T.astype(BF)
        dq_ref[own, :] = (dot32(keys_t, grad) * scale_q).T.astype(BF)
        dk_ref[own, :] = dk[:pair]
        dv_ref[own, :] = dv[:pair]
        dk1[g ^ 1] = dk[pair : pair + LEAF]
        dv1[g ^ 1] = dv[pair : pair + LEAF]
        dkx = dk[pair + LEAF :] if dkx is None else dkx + dk[pair + LEAF :]
        dvx = dv[pair + LEAF :] if dvx is None else dvx + dv[pair + LEAF :]
    r = lax.broadcasted_iota(jnp.int32, (pair, LEAF), 0)
    c = lax.broadcasted_iota(jnp.int32, (pair, LEAF), 1)
    expand = jnp.where(r // 2 == c, 0.5, 0.0).astype(BF)
    for g in range(groups):
        own = slice(g * pair, (g + 1) * pair)
        for ref, upper in ((dk_ref, dk1[g]), (dv_ref, dv1[g])):
            high = upper.astype(BF)
            low = (upper - high.astype(F32)).astype(BF)
            ref[own, :] += dot32(expand, high) + dot32(expand, low)
    dkx_ref[...] = dkx.astype(BF)
    dvx_ref[...] = dvx.astype(BF)


def fused_attention(q, k, v, do, kv1, kvx):
    tok_rows, cols = q.shape
    heads = cols // DH
    cross_rows = kvx.shape[0]

    def spec(rows, shift=0):
        return pl.BlockSpec((rows, DH), lambda h: (0, h + shift))

    out_shape = [
        jax.ShapeDtypeStruct((tok_rows, cols), BF),
        jax.ShapeDtypeStruct((tok_rows, cols), BF),
        jax.ShapeDtypeStruct((tok_rows, cols), F32),
        jax.ShapeDtypeStruct((tok_rows, cols), F32),
        jax.ShapeDtypeStruct((cross_rows, cols), BF),
        jax.ShapeDtypeStruct((cross_rows, cols), BF),
    ]
    scores = tok_rows * (3 * LEAF + cross_rows) * heads
    return pl.pallas_call(
        functools.partial(attention_kernel, tok_rows, cross_rows),
        grid=(heads,),
        in_specs=[spec(tok_rows)] * 4
        + [spec(kv1.shape[0]), spec(kv1.shape[0], heads)]
        + [spec(cross_rows), spec(cross_rows, heads)],
        out_specs=[spec(tok_rows)] * 4 + [spec(cross_rows)] * 2,
        out_shape=out_shape,
        compiler_params=pltpu.CompilerParams(vmem_limit_bytes=48 << 20),
        cost_estimate=pl.CostEstimate(
            flops=12 * scores * DH, bytes_accessed=16 * tok_rows * cols, transcendentals=2 * scores
        ),
        name="attention",
    )(q, k, v, do, kv1, kv1, kvx, kvx)


def cross_rows_of(apart):
    return LEAF >> (apart.bit_length() - 1)


def upper_matrix(tok_rows, seq_count):
    parts = []
    for apart in range(1, seq_count):
        count = cross_rows_of(apart)
        wide = tok_rows // count
        parts.append(np.kron(np.eye(count), np.ones((wide, 1))) / wide)
    return jnp.asarray(np.concatenate(parts, axis=1), BF)


def body(tokens, cotangent, w_query, w_key, w_value, w_out, seeds):
    seq_count = lax.axis_size("seq")
    head_count = lax.axis_size("head")
    seq_bits = seq_count.bit_length() - 1
    seq_idx = lax.axis_index("seq")
    head_idx = lax.axis_index("head")
    tok_rows, model_width = tokens.shape
    head_cols = w_query.shape[1]
    outer = seq_count // 2
    share = model_width // seq_count
    inner_idx = seq_idx % 2
    outer_idx = seq_idx // 2

    def swapped(array, axis, apart):
        return lax.ppermute(
            array, axis, [(i, i ^ apart) for i in range(lax.axis_size(axis))]
        )

    def half_of(array, which):
        view = array.reshape(tok_rows, outer, 2, share)
        return jnp.where(which == 0, view[:, :, 0], view[:, :, 1]).reshape(tok_rows, outer * share)

    tok_mine, cot_mine = half_of(tokens, inner_idx), half_of(cotangent, inner_idx)
    tok_pair = swapped(half_of(tokens, 1 - inner_idx), "seq", 1)
    cot_pair = swapped(half_of(cotangent, 1 - inner_idx), "seq", 1)

    all_ids = jnp.arange(model_width, dtype=jnp.int32)
    own_ids = head_idx * head_cols + jnp.arange(head_cols, dtype=jnp.int32)

    def over_lanes(vector):
        return jnp.broadcast_to(vector[:, None], (vector.shape[0], LANES))

    def hash_rows(ids):
        return over_lanes(centre(ids * 7919 % prime_mod))

    def hash_cols(ids, seed):
        seeded = (ids * 10007 % prime_mod + seed * 31337 % prime_mod) % prime_mod
        return centre(seeded)[None, :]

    all_hash, all_rows = hash_rows(all_ids), over_lanes(all_ids)
    own_hash, own_rows = hash_rows(own_ids), over_lanes(own_ids)

    def perturb_in(weight, n):
        return perturb(
            weight, all_hash, all_rows, hash_cols(own_ids, seeds[n]), own_ids[None, :], 0
        )

    key_w = perturb_in(w_key, 1)
    value_w = perturb_in(w_value, 2)
    keys = dot32(tokens, key_w).astype(BF)
    values = dot32(tokens, value_w).astype(BF)

    levels = 1 + seq_bits
    coarse = pl.pallas_call(
        coarse_kernel,
        out_shape=[
            jax.ShapeDtypeStruct((tok_rows >> n + 1, 2 * head_cols), BF) for n in range(levels)
        ],
        name="coarse",
    )(keys, values)
    kvx = jnp.concatenate(
        [swapped(coarse[d.bit_length()], "seq", d) for d in range(1, seq_count)], axis=0
    )

    query_w = perturb_in(w_query, 0)
    queries = dot32(tokens, query_w).astype(BF)
    out_w = perturb(w_out, own_hash, own_rows, hash_cols(all_ids, seeds[3]), all_ids[None, :], 1)
    grad_att = lax.dot_general(
        cotangent, out_w, (((1,), (1,)), ((), ())), preferred_element_type=F32
    ).astype(BF)

    att, dq, dk_own, dv_own, dkx, dvx = fused_attention(
        queries, keys, values, grad_att, coarse[0], kvx
    )

    returned = []
    at = 0
    dkvx = jnp.concatenate([dkx, dvx], axis=1)
    for apart in range(1, seq_count):
        count = cross_rows_of(apart)
        returned.append(swapped(dkvx[at : at + count], "seq", apart))
        at += count

    dq_pair = swapped(dq, "seq", 1)
    att_pair = swapped(att, "seq", 1)

    def sum_heads(terms):
        def piece(apart):
            return lax.dynamic_slice_in_dim(
                terms, (head_idx ^ apart) * head_cols, head_cols, axis=1
            )

        total = piece(0)
        for apart in range(1, head_count):
            total = total + swapped(piece(apart).astype(BF), "head", apart).astype(F32)
        return total.astype(BF)

    def reduce_chain(left, left_pair, right, right_pair, flip):
        def chunk(n):
            n = jnp.clip(n, 0, outer - 1) * share
            a = lax.dynamic_slice_in_dim(left, n, share, axis=1)
            b = lax.dynamic_slice_in_dim(left_pair, n, share, axis=1)
            if flip:
                return dot_rows(right, a) + dot_rows(right_pair, b)
            return dot_rows(a, right) + dot_rows(b, right_pair)

        up = down = None
        for t in range(1, outer):
            up_part = chunk(outer_idx + outer - t)
            down_part = chunk(outer_idx + t - outer)
            if up is not None:
                up_part = up_part + up.astype(F32)
                down_part = down_part + down.astype(F32)
            up_pairs = [(2 * z + x, 2 * z + 2 + x) for z in range(t) for x in range(2)]
            down_pairs = [
                (2 * z + x, 2 * z - 2 + x) for z in range(outer - t, outer) for x in range(2)
            ]
            up = lax.ppermute(up_part.astype(BF), "seq", up_pairs)
            down = lax.ppermute(down_part.astype(BF), "seq", down_pairs)
        own = chunk(outer_idx)
        if up is not None:
            own = own + up.astype(F32) + down.astype(F32)
        return own

    grad_w_out = reduce_chain(cot_mine, cot_pair, att, att_pair, True)
    grad_w_query = reduce_chain(tok_mine, tok_pair, dq, dq_pair, False)
    attended = sum_heads(dot32(att, out_w))

    upper = dot32(upper_matrix(tok_rows, seq_count), jnp.concatenate(returned, axis=0))
    dk = (dk_own + upper[:, :head_cols]).astype(BF)
    dv = (dv_own + upper[:, head_cols:]).astype(BF)
    dk_pair = swapped(dk, "seq", 1)
    dv_pair = swapped(dv, "seq", 1)

    def back(grad, weight):
        return lax.dot_general(grad, weight, (((1,), (1,)), ((), ())), preferred_element_type=F32)

    grad_tokens = sum_heads(back(dq, query_w) + back(dk, key_w) + back(dv, value_w))
    grad_w_key = reduce_chain(tok_mine, tok_pair, dk, dk_pair, False)
    grad_w_value = reduce_chain(tok_mine, tok_pair, dv, dv_pair, False)
    return (attended, grad_tokens, grad_w_query, grad_w_key, grad_w_value, grad_w_out)


def solution(mesh):
    in_specs = (
        P("seq", None),
        P("seq", None),
        P(None, "head"),
        P(None, "head"),
        P(None, "head"),
        P("head", None),
        P(),
    )
    out_specs = (
        P("seq", "head"),
        P("seq", "head"),
        P("seq", "head"),
        P("seq", "head"),
        P("seq", "head"),
        P("head", "seq"),
    )
    return jax.shard_map(body, mesh=mesh, in_specs=in_specs, out_specs=out_specs, check_vma=False)
```

time: 702 us -> 273 us (0.39); the launches traced: 689 us -> 272 us
  waiting for transfers between devices: 339 us -> 77.8 us
  local copies, waits for them, and re-layouts: 143 us -> 22.7 us
  starting transfers between devices: 7.93 us -> 84.2 us
  other arithmetic: 76.6 us -> 7.81 us
  matrix products: 105 us -> 37.9 us
  Pallas kernels: 0 us -> 37.1 us
  between operations: 17.7 us -> 4.58 us
    reduce_scatter x3 -> x0, waiting for transfers between devices: 313 us -> none  [the longest x1 285 us: body(): lax.psum_scatter(jnp.concatenate([lax.dot_general(tokens, grads_cat, (((0...]
    ppermute x6 -> x50, starting transfers between devices: 7.81 us -> 84.2 us  [the longest x12 47.5 us: reduce_chain(): up = lax.ppermute(up_part.astype(BF), 'seq', up_pairs)]
    dot_general x46 -> x71, matrix products: 105 us -> 37.9 us  [the longest x56 20.9 us: dot_rows(): lax.dot_general(left, right, (((0,), (0,)), ((), ())), preferred_element_...]
    ppermute x6 -> x50, waiting for transfers between devices: 25.5 us -> 77.8 us  [the longest x26 75.9 us: swapped(): lax.ppermute(array, axis, [(i, i ^ apart) for i in range(lax.axis_size(ax...]
    convert_element_type x15 -> x3, other arithmetic: 47.8 us -> 2.75 us  [the longest x2 2.2 us: sum_heads(): return total.astype(BF)]
    pallas_call x0 -> x6, Pallas kernels: none -> 37.1 us  [the longest x4 23.2 us: perturb(): pl.pallas_call(functools.partial(perturb_kernel, axis_no), grid=(steps,),...]
    reshape x12 -> x0, local copies, waits for them, and re-layouts: 26.1 us -> none  [the longest x4 10.3 us: body(): numerator = numerator + part_num.reshape(head_shape)]
    another operation x14 -> x0, local copies, waits for them, and re-layouts: 18 us -> none  [the longest x7 9.73 us: group_view(): array_in.reshape((groups, array_in.shape[0] // groups) + array_in.shape[1:])]
  transfers between devices with their start and end apart: 9 -> 50, of which waited for: 5 -> 13; matrix products, arithmetic and copies ran while one was open for 28% -> 19% of each run, Pallas kernels for 0% -> 8%
where the time goes in v1:
time: 273 us; the launch traced here: 272 us
  starting transfers between devices  84.2 us (31%)
  waiting for transfers between devices  77.8 us (28%)
  matrix products  37.9 us (14%)
  Pallas kernels  37.1 us (14%)
  local copies, waits for them, and re-layouts  22.7 us (8%)
  other arithmetic  7.81 us (3%)
  between operations  4.58 us (2%)
    ppermute x26, waiting for transfers between devices, swapped(): lax.ppermute(array, axis, [(i, i ^ apart) for i in range(lax.axis_size(ax...  75.9 us
    ppermute x12, starting transfers between devices, reduce_chain(): up = lax.ppermute(up_part.astype(BF), 'seq', up_pairs)  47.5 us
    ppermute x26, starting transfers between devices, swapped(): lax.ppermute(array, axis, [(i, i ^ apart) for i in range(lax.axis_size(ax...  26.1 us
    pallas_call x4, Pallas kernels, perturb(): pl.pallas_call(functools.partial(perturb_kernel, axis_no), grid=(steps,),...  23.2 us
    dot_general x56, matrix products, dot_rows(): lax.dot_general(left, right, (((0,), (0,)), ((), ())), preferred_element_...  20.9 us
    unnamed x65, local copies, waits for them, and re-layouts  19.9 us
    dot_general x11, matrix products, dot32(): return jnp.dot(left, right, preferred_element_type=F32)  10.8 us
    pallas_call x1, Pallas kernels, fused_attention(): pl.pallas_call(functools.partial(attention_kernel, tok_rows, cross_rows),...  10.7 us
  transfers between devices with their start and end apart: 50, of which 13 were waited for; matrix products, arithmetic and copies ran while one was open for 19% of the time, Pallas kernels for 8%

profile of v1, /device:TPU:0, one launch (start us, length us, event | category | flops | bytes accessed | tf_op | source)
XLA Modules:
  0.0 272.1 jit_solution(5030991080321814916)
XLA Ops:
  4.0 6.2 %perturb.5 = bf16[2048,512]{1,0:T(8,128)(2,1)S(1)} custom-call(s32[2048,128]{1,0:T(8,128)S(1)} %broadcast_in_dim.16.row_hash, s32[2048,128]{1,0:T(8,128)S(1)} %broadcast_in_dim.18.row_id, s32[1,512]{1,0:T(1,128)S(1)} %get-tuple-element.49.col_hash, s32[1,512]{1,0:T(1,128)S(1)} %iota_add_fusion.1.col_id, bf16[2048,512]{1,0:T(8,128)(2,1)S(1)} %copy-done.7), custom_call_target="tpu_custom_call" | custom-call | flops 31457280 | bytes 4194304 | tf_op jit(solution)/shard_map/perturb/pallas_call | solution.py:90
  12.7 6.2 %perturb.6 = bf16[2048,512]{1,0:T(8,128)(2,1)S(1)} custom-call(s32[2048,128]{1,0:T(8,128)S(1)} %broadcast_in_dim.16.row_hash, s32[2048,128]{1,0:T(8,128)S(1)} %broadcast_in_dim.19.row_id, s32[1,512]{1,0:T(1,128)S(1)} %get-tuple-element.48.col_hash, s32[1,512]{1,0:T(1,128)S(1)} %iota_add_fusion.1.col_id, bf16[2048,512]{1,0:T(8,128)(2,1)S(1)} %copy-done.8), custom_call_target="tpu_custom_call" | custom-call | flops 31457280 | bytes 4194304 | tf_op jit(solution)/shard_map/perturb/pallas_call | solution.py:90
  22.3 3.1 %coarse.1 = (bf16[256,1024]{1,0:T(8,128)(2,1)}, bf16[128,1024]{1,0:T(8,128)(2,1)}, bf16[64,1024]{1,0:T(8,128)(2,1)}, bf16[32,1024]{1,0:T(8,128)(2,1)}) custom-call(bf16[512,512]{1,0:T(8,128)(2,1)} %fusion.2.k_ref, bf16[512,512]{1,0:T(8,128)(2,1)} %fusion.3.v_ref), custom_call_target="tpu_custom_call" | custom-call | tf_op jit(solution)/shard_map/coarse/pallas_call | solution.py:290
  25.5 3.0 %collective-permute-start.1 = (bf16[64,1024]{1,0:T(8,128)(2,1)}, bf16[64,1024]{1,0:T(8,128)(2,1)}, u32[]{:S(2)}, u32[]{:S(2)}) collective-permute-start(bf16[64,1024]{1,0:T(8,128)(2,1)} %get-tuple-element.18), channel_id=1, source_target_pairs={{0,8},{4,12},{8,0},{12,4},{16,24},{20,28},{24,16},{28,20},{1,9},{5... | collective-permute-start | bytes 393224 | tf_op jit(solution)/shard_map/ppermute | solution.py:251
  29.9 2.6 collective-permute-start.3
  35.6 4.1 %copy.47 = bf16[512,2048]{0,1:T(8,128)(2,1)} copy(bf16[512,2048]{1,0:T(8,128)(2,1)} %param.8) | data formatting | bytes 4194304 | tf_op args[0]
  39.9 6.2 %perturb.4 = bf16[2048,512]{1,0:T(8,128)(2,1)S(1)} custom-call(s32[2048,128]{1,0:T(8,128)S(1)} %broadcast_in_dim.16.row_hash, s32[2048,128]{1,0:T(8,128)S(1)} %broadcast_in_dim.17.row_id, s32[1,512]{1,0:T(1,128)S(1)} %compare_select_fusion.4.col_hash, s32[1,512]{1,0:T(1,128)S(1)} %iota_add_fusion.1.col_id, bf16[2048,512]{1,0:T(8,128)(2,1)S(1)} %copy-done.9), custom_call_target="tpu_custom_call" | custom-call | flops 31457280 | bytes 4194304 | tf_op jit(solution)/shard_map/perturb/pallas_call | solution.py:90
  49.6 2.5 copy.48
  53.9 4.7 %perturb.7 = bf16[512,2048]{1,0:T(8,128)(2,1)S(1)} custom-call(s32[512,128]{1,0:T(8,128)S(1)} %broadcast_in_dim.20.row_hash, s32[512,128]{1,0:T(8,128)S(1)} %broadcast_in_dim.21.row_id, s32[1,2048]{1,0:T(1,128)S(1)} %compare_select_fusion.col_hash, s32[1,2048]{1,0:T(1,128)S(1)} %iota.35.col_id, bf16[512,2048]{1,0:T(8,128)(2,1)S(1)} %copy-done.6), custom_call_target="tpu_custom_call" | custom-call | flops 31457280 | bytes 4194304 | tf_op jit(solution)/shard_map/perturb/pallas_call | solution.py:90
  60.7 3.3 %broadcast_select_fusion.3 = (bf16[512,4,1,256]{0,3,2,1:T(8,128)(2,1)}, bf16[512,4,1,256]{0,3,2,1:T(8,128)(2,1)}) fusion(pred[]{:T(512)S(6)} %eq.26, bf16[512,4,2,256]{0,3,2,1:T(8,128)(2,1)} %bitcast.127, pred[]{:T(512)S(6)} %eq.27), kind=kLoop, calls=%fused_computation.101 | loop fusion | flops 1048576 | bytes 4194306 | tf_op jit(solution)/shard_map/jit(_where)/select_n | solution.py:257
  65.6 3.6 %collective-permute-start.5 = (bf16[32,1024]{1,0:T(8,128)(2,1)}, bf16[32,1024]{1,0:T(8,128)(2,1)S(1)}, u32[]{:S(2)}, u32[]{:S(2)}) collective-permute-start(bf16[32,1024]{1,0:T(8,128)(2,1)} %get-tuple-element.19), channel_id=1, source_target_pairs={{0,24},{4,28},{8,16},{12,20},{16,8},{20,12},{24,0},{28,4},{1,25},{... | collective-permute-start | bytes 196616 | tf_op jit(solution)/shard_map/ppermute | solution.py:251
  73.7 2.9 %collective-permute-done.6 = bf16[32,1024]{1,0:T(8,128)(2,1)S(1)} collective-permute-done((bf16[32,1024]{1,0:T(8,128)(2,1)}, bf16[32,1024]{1,0:T(8,128)(2,1)S(1)}, u32[]{:S(2)}, u32[]{:S(2)}) %collective-permute-start.6) | collective-permute-done | bytes 65568 | tf_op jit(solution)/shard_map/ppermute | solution.py:251
  79.7 10.7 %attention.1 = (bf16[512,512]{1,0:T(8,128)(2,1)S(1)}, bf16[512,512]{1,0:T(8,128)(2,1)S(1)}, f32[512,512]{1,0:T(8,128)}, f32[512,512]{1,0:T(8,128)}, bf16[384,512...) custom-call(bf16[512,512]{1,0:T(8,128)(2,1)S(1)} %copy-done.13, bf16[512,512]{1,0:T(8,128)(2,1)S(1)} %copy-done.10, ...), custom_call_target="tpu_custom_call" | custom-call | flops 2415919104 | bytes 4194304 | tf_op jit(solution)/shard_map/attention/pallas_call | solution.py:208
  94.9 3.1 %collective-permute-done.15 = bf16[32,1024]{1,0:T(8,128)(2,1)S(1)} collective-permute-done((bf16[32,1024]{1,0:T(8,128)(2,1)S(1)}, bf16[32,1024]{1,0:T(8,128)(2,1)S(1)}, u32[]{:S(2)}, u32[]{:S(2)}) %collective-permute-start.15) | collective-permute-done | bytes 65568 | tf_op jit(solution)/shard_map/ppermute | solution.py:251
  98.4 5.7 %collective-permute-done.14 = bf16[32,1024]{1,0:T(8,128)(2,1)S(1)} collective-permute-done((bf16[32,1024]{1,0:T(8,128)(2,1)S(1)}, bf16[32,1024]{1,0:T(8,128)(2,1)S(1)}, u32[]{:S(2)}, u32[]{:S(2)}) %collective-permute-start.14) | collective-permute-done | bytes 65568 | tf_op jit(solution)/shard_map/ppermute | solution.py:251
  104.5 4.9 %collective-permute-done.13 = bf16[32,1024]{1,0:T(8,128)(2,1)S(1)} collective-permute-done((bf16[32,1024]{1,0:T(8,128)(2,1)S(1)}, bf16[32,1024]{1,0:T(8,128)(2,1)S(1)}, u32[]{:S(2)}, u32[]{:S(2)}) %collective-permute-start.13) | collective-permute-done | bytes 65568 | tf_op jit(solution)/shard_map/ppermute | solution.py:251
  109.8 6.4 %collective-permute-done.12 = bf16[64,1024]{1,0:T(8,128)(2,1)S(1)} collective-permute-done((bf16[64,1024]{1,0:T(8,128)(2,1)S(1)}, bf16[64,1024]{1,0:T(8,128)(2,1)S(1)}, u32[]{:S(2)}, u32[]{:S(2)}) %collective-permute-start.12) | collective-permute-done | bytes 131104 | tf_op jit(solution)/shard_map/ppermute | solution.py:251
  116.5 4.6 %collective-permute-done.11 = bf16[64,1024]{1,0:T(8,128)(2,1)S(1)} collective-permute-done((bf16[64,1024]{1,0:T(8,128)(2,1)S(1)}, bf16[64,1024]{1,0:T(8,128)(2,1)S(1)}, u32[]{:S(2)}, u32[]{:S(2)}) %collective-permute-start.11) | collective-permute-done | bytes 131104 | tf_op jit(solution)/shard_map/ppermute | solution.py:251
  122.3 5.9 %collective-permute-done.10 = bf16[128,1024]{1,0:T(8,128)(2,1)S(1)} collective-permute-done((bf16[128,1024]{1,0:T(8,128)(2,1)S(1)}, bf16[128,1024]{1,0:T(8,128)(2,1)S(1)}, u32[]{:S(2)}, u32[]{:S(2)}) %collective-permute-start.10) | collective-permute-done | bytes 262176 | tf_op jit(solution)/shard_map/ppermute | solution.py:251
  130.5 4.7 %collective-permute-done.16 = bf16[32,1024]{1,0:T(8,128)(2,1)S(1)} collective-permute-done((bf16[32,1024]{1,0:T(8,128)(2,1)S(1)}, bf16[32,1024]{1,0:T(8,128)(2,1)S(1)}, u32[]{:S(2)}, u32[]{:S(2)}) %collective-permute-start.16) | collective-permute-done | bytes 65568 | tf_op jit(solution)/shard_map/ppermute | solution.py:251
  156.9 29.2 %collective-permute-done.42 = bf16[512,512]{1,0:T(8,128)(2,1)S(1)} collective-permute-done((bf16[512,512]{1,0:T(8,128)(2,1)S(1)}, bf16[512,512]{1,0:T(8,128)(2,1)S(1)}, u32[]{:S(2)}, u32[]{:S(2)}) %collective-permute-start.42) | collective-permute-done | bytes 524320 | tf_op jit(solution)/shard_map/ppermute | solution.py:251
  190.0 4.9 %collective-permute-done.28 = bf16[512,512]{1,0:T(8,128)(2,1)S(1)} collective-permute-done((bf16[512,512]{1,0:T(8,128)(2,1)S(1)}, bf16[512,512]{1,0:T(8,128)(2,1)S(1)}, u32[]{:S(2)}, u32[]{:S(2)}) %collective-permute-start.28) | collective-permute-done | bytes 524320 | tf_op jit(solution)/shard_map/ppermute | solution.py:251
  197.0 3.6 %collective-permute-done.35 = bf16[512,512]{1,0:T(8,128)(2,1)S(1)} collective-permute-done((bf16[512,512]{1,0:T(8,128)(2,1)S(1)}, bf16[512,512]{1,0:T(8,128)(2,1)S(1)}, u32[]{:S(2)}, u32[]{:S(2)}) %collective-permute-start.35) | collective-permute-done | bytes 524320 | tf_op jit(solution)/shard_map/ppermute | solution.py:251
  209.6 4.4 %collective-permute-start.44 = (bf16[512,256]{1,0:T(8,128)(2,1)S(1)}, bf16[512,256]{1,0:T(8,128)(2,1)S(1)}, u32[]{:S(2)}, u32[]{:S(2)}) collective-permute-start(bf16[512,256]{1,0:T(8,128)(2,1)S(1)} %fusion.50), channel_id=1, source_target_pairs={{0,8},{4,12},{1,9},{5,13},{2,10},{6,14},{3,11},{7,15}} | collective-permute-start | bytes 786440 | tf_op jit(solution)/shard_map/ppermute | solution.py:354
  215.4 4.9 %collective-permute-start.23 = (bf16[256,512]{1,0:T(8,128)(2,1)S(1)}, bf16[256,512]{1,0:T(8,128)(2,1)S(1)}, u32[]{:S(2)}, u32[]{:S(2)}) collective-permute-start(bf16[256,512]{1,0:T(8,128)(2,1)S(1)} %fusion.29), channel_id=1, source_target_pairs={{0,8},{4,12},{8,16},{12,20},{1,9},{5,13},{9,17},{13,21},{2,10},{6,... | collective-permute-start | bytes 786440 | tf_op jit(solution)/shard_map/ppermute | solution.py:354
  221.6 5.2 %collective-permute-start.30 = (bf16[256,512]{1,0:T(8,128)(2,1)S(1)}, bf16[256,512]{1,0:T(8,128)(2,1)S(1)}, u32[]{:S(2)}, u32[]{:S(2)}) collective-permute-start(bf16[256,512]{1,0:T(8,128)(2,1)S(1)} %fusion.33), channel_id=1, source_target_pairs={{0,8},{4,12},{8,16},{12,20},{1,9},{5,13},{9,17},{13,21},{2,10},{6,... | collective-permute-start | bytes 786440 | tf_op jit(solution)/shard_map/ppermute | solution.py:354
  228.2 5.2 %collective-permute-start.37 = (bf16[256,512]{1,0:T(8,128)(2,1)S(1)}, bf16[256,512]{1,0:T(8,128)(2,1)S(1)}, u32[]{:S(2)}, u32[]{:S(2)}) collective-permute-start(bf16[256,512]{1,0:T(8,128)(2,1)S(1)} %fusion.37), channel_id=1, source_target_pairs={{0,8},{4,12},{8,16},{12,20},{1,9},{5,13},{9,17},{13,21},{2,10},{6,... | collective-permute-start | bytes 786440 | tf_op jit(solution)/shard_map/ppermute | solution.py:354
  234.7 5.2 %collective-permute-start.45 = (bf16[512,256]{1,0:T(8,128)(2,1)S(1)}, bf16[512,256]{1,0:T(8,128)(2,1)S(1)}, u32[]{:S(2)}, u32[]{:S(2)}) collective-permute-start(bf16[512,256]{1,0:T(8,128)(2,1)S(1)} %fusion.41), channel_id=1, source_target_pairs={{0,8},{4,12},{8,16},{12,20},{1,9},{5,13},{9,17},{13,21},{2,10},{6,... | collective-permute-start | bytes 786440 | tf_op jit(solution)/shard_map/ppermute | solution.py:354
  241.8 5.2 %collective-permute-start.24 = (bf16[256,512]{1,0:T(8,128)(2,1)S(1)}, bf16[256,512]{1,0:T(8,128)(2,1)S(1)}, u32[]{:S(2)}, u32[]{:S(2)}) collective-permute-start(bf16[256,512]{1,0:T(8,128)(2,1)S(1)} %fusion.28), channel_id=1, source_target_pairs={{0,8},{4,12},{8,16},{12,20},{16,24},{20,28},{1,9},{5,13},{9,17},{1... | collective-permute-start | bytes 786440 | tf_op jit(solution)/shard_map/ppermute | solution.py:354
  248.9 4.6 %collective-permute-start.31 = (bf16[256,512]{1,0:T(8,128)(2,1)S(1)}, bf16[256,512]{1,0:T(8,128)(2,1)S(1)}, u32[]{:S(2)}, u32[]{:S(2)}) collective-permute-start(bf16[256,512]{1,0:T(8,128)(2,1)S(1)} %fusion.32), channel_id=1, source_target_pairs={{0,8},{4,12},{8,16},{12,20},{16,24},{20,28},{1,9},{5,13},{9,17},{1... | collective-permute-start | bytes 786440 | tf_op jit(solution)/shard_map/ppermute | solution.py:354
  255.5 4.6 %collective-permute-start.38 = (bf16[256,512]{1,0:T(8,128)(2,1)S(1)}, bf16[256,512]{1,0:T(8,128)(2,1)S(1)}, u32[]{:S(2)}, u32[]{:S(2)}) collective-permute-start(bf16[256,512]{1,0:T(8,128)(2,1)S(1)} %fusion.36), channel_id=1, source_target_pairs={{0,8},{4,12},{8,16},{12,20},{16,24},{20,28},{1,9},{5,13},{9,17},{1... | collective-permute-start | bytes 786440 | tf_op jit(solution)/shard_map/ppermute | solution.py:354
  262.6 4.6 %collective-permute-start.46 = (bf16[512,256]{1,0:T(8,128)(2,1)S(1)}, bf16[512,256]{1,0:T(8,128)(2,1)S(1)}, u32[]{:S(2)}, u32[]{:S(2)}) collective-permute-start(bf16[512,256]{1,0:T(8,128)(2,1)S(1)} %fusion.40), channel_id=1, source_target_pairs={{0,8},{4,12},{8,16},{12,20},{16,24},{20,28},{1,9},{5,13},{9,17},{1... | collective-permute-start | bytes 786440 | tf_op jit(solution)/shard_map/ppermute | solution.py:354
  (236 shorter events, 91.8 us)
Async XLA Ops:
  25.5 43.7 %collective-permute-start.1 = (bf16[64,1024]{1,0:T(8,128)(2,1)}, bf16[64,1024]{1,0:T(8,128)(2,1)}, u32[]{:S(2)}, u32[]{:S(2)}) collective-permute-start(bf16[64,1024]{1,0:T(8,128)(2,1)} %get-tuple-element.18), channel_id=1, source_target_pairs={{0,8},{4,12},{8,0},{12,4},{16,24},{20,28},{24,16},{28,20},{1,9},{5... | collective-permute-start | bytes 393224 | tf_op jit(solution)/shard_map/ppermute | solution.py:251
  28.5 41.7 %collective-permute-start.2 = (bf16[64,1024]{1,0:T(8,128)(2,1)}, bf16[64,1024]{1,0:T(8,128)(2,1)S(1)}, u32[]{:S(2)}, u32[]{:S(2)}) collective-permute-start(bf16[64,1024]{1,0:T(8,128)(2,1)} %get-tuple-element.18), channel_id=1, source_target_pairs={{0,12},{4,8},{8,4},{12,0},{16,28},{20,24},{24,20},{28,16},{1,13},{... | collective-permute-start | bytes 393224 | tf_op jit(solution)/shard_map/ppermute | solution.py:251
  29.9 42.1 %collective-permute-start.3 = (bf16[32,1024]{1,0:T(8,128)(2,1)}, bf16[32,1024]{1,0:T(8,128)(2,1)}, u32[]{:S(2)}, u32[]{:S(2)}) collective-permute-start(bf16[32,1024]{1,0:T(8,128)(2,1)} %get-tuple-element.19), channel_id=1, source_target_pairs={{0,16},{4,20},{8,24},{12,28},{16,0},{20,4},{24,8},{28,12},{1,17},{... | collective-permute-start | bytes 196616 | tf_op jit(solution)/shard_map/ppermute | solution.py:251
  32.5 40.3 %collective-permute-start.4 = (bf16[32,1024]{1,0:T(8,128)(2,1)}, bf16[32,1024]{1,0:T(8,128)(2,1)}, u32[]{:S(2)}, u32[]{:S(2)}) collective-permute-start(bf16[32,1024]{1,0:T(8,128)(2,1)} %get-tuple-element.19), channel_id=1, source_target_pairs={{0,20},{4,16},{8,28},{12,24},{16,4},{20,0},{24,12},{28,8},{1,21},{... | collective-permute-start | bytes 196616 | tf_op jit(solution)/shard_map/ppermute | solution.py:251
  32.5 33.1 %collective-permute-start = (bf16[128,1024]{1,0:T(8,128)(2,1)}, bf16[128,1024]{1,0:T(8,128)(2,1)S(1)}, u32[]{:S(2)}, u32[]{:S(2)}) collective-permute-start(bf16[128,1024]{1,0:T(8,128)(2,1)} %get-tuple-element.17), channel_id=1, source_target_pairs={{0,4},{4,0},{8,12},{12,8},{16,20},{20,16},{24,28},{28,24},{1,5},{5... | collective-permute-start | bytes 786440 | tf_op jit(solution)/shard_map/ppermute | solution.py:251
  70.2 83.7 %collective-permute-start.20 = (bf16[512,1024]{0,1:T(8,128)(2,1)}, bf16[512,1024]{0,1:T(8,128)(2,1)S(1)}, u32[]{:S(2)}, u32[]{:S(2)}) collective-permute-start(bf16[512,1024]{0,1:T(8,128)(2,1)} %bitcast.137), channel_id=1, source_target_pairs={{0,4},{4,0},{8,12},{12,8},{16,20},{20,16},{24,28},{28,24},{1,5},{5... | collective-permute-start | bytes 3145736 | tf_op jit(solution)/shard_map/ppermute | solution.py:251
  92.9 55.2 %collective-permute-start.9 = (bf16[512,512]{1,0:T(8,128)(2,1)S(1)}, bf16[512,512]{1,0:T(8,128)(2,1)S(1)}, u32[]{:S(2)}, u32[]{:S(2)}) collective-permute-start(bf16[512,512]{1,0:T(8,128)(2,1)S(1)} %get-tuple-element.30), channel_id=1, source_target_pairs={{0,3},{1,2},{2,1},{3,0},{4,7},{5,6},{6,5},{7,4},{8,11},{9,10},{10,... | collective-permute-start | bytes 1572872 | tf_op jit(solution)/shard_map/ppermute | solution.py:251
  93.0 57.0 %collective-permute-start.8 = (bf16[512,512]{1,0:T(8,128)(2,1)S(1)}, bf16[512,512]{1,0:T(8,128)(2,1)S(1)}, u32[]{:S(2)}, u32[]{:S(2)}) collective-permute-start(bf16[512,512]{1,0:T(8,128)(2,1)S(1)} %get-tuple-element.31), channel_id=1, source_target_pairs={{0,2},{1,3},{2,0},{3,1},{4,6},{5,7},{6,4},{7,5},{8,10},{9,11},{10,... | collective-permute-start | bytes 1572872 | tf_op jit(solution)/shard_map/ppermute | solution.py:251
  94.6 56.2 %collective-permute-start.7 = (bf16[512,512]{1,0:T(8,128)(2,1)S(1)}, bf16[512,512]{1,0:T(8,128)(2,1)S(1)}, u32[]{:S(2)}, u32[]{:S(2)}) collective-permute-start(bf16[512,512]{1,0:T(8,128)(2,1)S(1)} %get-tuple-element.29), channel_id=1, source_target_pairs={{0,1},{1,0},{2,3},{3,2},{4,5},{5,4},{6,7},{7,6},{8,9},{9,8},{10,11... | collective-permute-start | bytes 1572872 | tf_op jit(solution)/shard_map/ppermute | solution.py:251
  135.2 17.9 %collective-permute-start.21 = (bf16[512,512]{1,0:T(8,128)(2,1)S(1)}, bf16[512,512]{1,0:T(8,128)(2,1)S(1)}, u32[]{:S(2)}, u32[]{:S(2)}) collective-permute-start(bf16[512,512]{1,0:T(8,128)(2,1)S(1)} %get-tuple-element.21), channel_id=1, source_target_pairs={{0,4},{4,0},{8,12},{12,8},{16,20},{20,16},{24,28},{28,24},{1,5},{5... | collective-permute-start | bytes 1572872 | tf_op jit(solution)/shard_map/ppermute | solution.py:251
  148.8 39.0 %collective-permute-start.43 = (bf16[512,1024]{0,1:T(8,128)(2,1)S(1)}, bf16[512,1024]{0,1:T(8,128)(2,1)S(1)}, u32[]{:S(2)}, u32[]{:S(2)}) collective-permute-start(bf16[512,1024]{0,1:T(8,128)(2,1)S(1)} %bitcast.136), channel_id=1, source_target_pairs={{0,4},{4,0},{8,12},{12,8},{16,20},{20,16},{24,28},{28,24},{1,5},{5... | collective-permute-start | bytes 3145736 | tf_op jit(solution)/shard_map/ppermute | solution.py:251
  150.0 36.1 %collective-permute-start.42 = (bf16[512,512]{1,0:T(8,128)(2,1)S(1)}, bf16[512,512]{1,0:T(8,128)(2,1)S(1)}, u32[]{:S(2)}, u32[]{:S(2)}) collective-permute-start(bf16[512,512]{1,0:T(8,128)(2,1)S(1)} %get-tuple-element.20), channel_id=1, source_target_pairs={{0,4},{4,0},{8,12},{12,8},{16,20},{20,16},{24,28},{28,24},{1,5},{5... | collective-permute-start | bytes 1572872 | tf_op jit(solution)/shard_map/ppermute | solution.py:251
  150.8 44.2 %collective-permute-start.28 = (bf16[512,512]{1,0:T(8,128)(2,1)S(1)}, bf16[512,512]{1,0:T(8,128)(2,1)S(1)}, u32[]{:S(2)}, u32[]{:S(2)}) collective-permute-start(bf16[512,512]{1,0:T(8,128)(2,1)S(1)} %get-tuple-element.36), channel_id=1, source_target_pairs={{0,4},{4,0},{8,12},{12,8},{16,20},{20,16},{24,28},{28,24},{1,5},{5... | collective-permute-start | bytes 1572872 | tf_op jit(solution)/shard_map/ppermute | solution.py:251
  153.1 47.5 %collective-permute-start.35 = (bf16[512,512]{1,0:T(8,128)(2,1)S(1)}, bf16[512,512]{1,0:T(8,128)(2,1)S(1)}, u32[]{:S(2)}, u32[]{:S(2)}) collective-permute-start(bf16[512,512]{1,0:T(8,128)(2,1)S(1)} %get-tuple-element.37), channel_id=1, source_target_pairs={{0,4},{4,0},{8,12},{12,8},{16,20},{20,16},{24,28},{28,24},{1,5},{5... | collective-permute-start | bytes 1572872 | tf_op jit(solution)/shard_map/ppermute | solution.py:251
  153.9 48.3 %collective-permute-start.19 = (bf16[512,512]{1,0:T(8,128)(2,1)S(1)}, bf16[512,512]{1,0:T(8,128)(2,1)S(1)}, u32[]{:S(2)}, u32[]{:S(2)}) collective-permute-start(bf16[512,512]{1,0:T(8,128)(2,1)S(1)} %get-tuple-element.27), channel_id=1, source_target_pairs={{0,3},{1,2},{2,1},{3,0},{4,7},{5,6},{6,5},{7,4},{8,11},{9,10},{10,... | collective-permute-start | bytes 1572872 | tf_op jit(solution)/shard_map/ppermute | solution.py:251
  186.1 16.8 %collective-permute-start.18 = (bf16[512,512]{1,0:T(8,128)(2,1)S(1)}, bf16[512,512]{1,0:T(8,128)(2,1)S(1)}, u32[]{:S(2)}, u32[]{:S(2)}) collective-permute-start(bf16[512,512]{1,0:T(8,128)(2,1)S(1)} %get-tuple-element.28), channel_id=1, source_target_pairs={{0,2},{1,3},{2,0},{3,1},{4,6},{5,7},{6,4},{7,5},{8,10},{9,11},{10,... | collective-permute-start | bytes 1572872 | tf_op jit(solution)/shard_map/ppermute | solution.py:251
  187.7 16.5 %collective-permute-start.17 = (bf16[512,512]{1,0:T(8,128)(2,1)S(1)}, bf16[512,512]{1,0:T(8,128)(2,1)S(1)}, u32[]{:S(2)}, u32[]{:S(2)}) collective-permute-start(bf16[512,512]{1,0:T(8,128)(2,1)S(1)} %get-tuple-element.26), channel_id=1, source_target_pairs={{0,1},{1,0},{2,3},{3,2},{4,5},{5,4},{6,7},{7,6},{8,9},{9,8},{10,11... | collective-permute-start | bytes 1572872 | tf_op jit(solution)/shard_map/ppermute | solution.py:251
  206.7 13.9 %collective-permute-start.36 = (bf16[256,512]{1,0:T(8,128)(2,1)S(1)}, bf16[256,512]{1,0:T(8,128)(2,1)S(1)}, u32[]{:S(2)}, u32[]{:S(2)}) collective-permute-start(bf16[256,512]{1,0:T(8,128)(2,1)S(1)} %fusion.48), channel_id=1, source_target_pairs={{0,8},{4,12},{1,9},{5,13},{2,10},{6,14},{3,11},{7,15}} | collective-permute-start | bytes 786440 | tf_op jit(solution)/shard_map/ppermute | solution.py:354
  209.6 17.5 %collective-permute-start.44 = (bf16[512,256]{1,0:T(8,128)(2,1)S(1)}, bf16[512,256]{1,0:T(8,128)(2,1)S(1)}, u32[]{:S(2)}, u32[]{:S(2)}) collective-permute-start(bf16[512,256]{1,0:T(8,128)(2,1)S(1)} %fusion.50), channel_id=1, source_target_pairs={{0,8},{4,12},{1,9},{5,13},{2,10},{6,14},{3,11},{7,15}} | collective-permute-start | bytes 786440 | tf_op jit(solution)/shard_map/ppermute | solution.py:354
  214.4 13.8 %collective-permute-start.26 = (bf16[256,512]{1,0:T(8,128)(2,1)S(1)}, bf16[256,512]{1,0:T(8,128)(2,1)S(1)}, u32[]{:S(2)}, u32[]{:S(2)}) collective-permute-start(bf16[256,512]{1,0:T(8,128)(2,1)S(1)} %fusion.31), channel_id=1, source_target_pairs={{16,8},{20,12},{24,16},{28,20},{17,9},{21,13},{25,17},{29,21},{18,... | collective-permute-start | bytes 786440 | tf_op jit(solution)/shard_map/ppermute | solution.py:355
  215.4 18.3 %collective-permute-start.23 = (bf16[256,512]{1,0:T(8,128)(2,1)S(1)}, bf16[256,512]{1,0:T(8,128)(2,1)S(1)}, u32[]{:S(2)}, u32[]{:S(2)}) collective-permute-start(bf16[256,512]{1,0:T(8,128)(2,1)S(1)} %fusion.29), channel_id=1, source_target_pairs={{0,8},{4,12},{8,16},{12,20},{1,9},{5,13},{9,17},{13,21},{2,10},{6,... | collective-permute-start | bytes 786440 | tf_op jit(solution)/shard_map/ppermute | solution.py:354
  220.6 14.1 %collective-permute-start.33 = (bf16[256,512]{1,0:T(8,128)(2,1)S(1)}, bf16[256,512]{1,0:T(8,128)(2,1)S(1)}, u32[]{:S(2)}, u32[]{:S(2)}) collective-permute-start(bf16[256,512]{1,0:T(8,128)(2,1)S(1)} %fusion.35), channel_id=1, source_target_pairs={{16,8},{20,12},{24,16},{28,20},{17,9},{21,13},{25,17},{29,21},{18,... | collective-permute-start | bytes 786440 | tf_op jit(solution)/shard_map/ppermute | solution.py:355
  221.6 18.6 %collective-permute-start.30 = (bf16[256,512]{1,0:T(8,128)(2,1)S(1)}, bf16[256,512]{1,0:T(8,128)(2,1)S(1)}, u32[]{:S(2)}, u32[]{:S(2)}) collective-permute-start(bf16[256,512]{1,0:T(8,128)(2,1)S(1)} %fusion.33), channel_id=1, source_target_pairs={{0,8},{4,12},{8,16},{12,20},{1,9},{5,13},{9,17},{13,21},{2,10},{6,... | collective-permute-start | bytes 786440 | tf_op jit(solution)/shard_map/ppermute | solution.py:354
  227.1 14.6 %collective-permute-start.40 = (bf16[256,512]{1,0:T(8,128)(2,1)S(1)}, bf16[256,512]{1,0:T(8,128)(2,1)S(1)}, u32[]{:S(2)}, u32[]{:S(2)}) collective-permute-start(bf16[256,512]{1,0:T(8,128)(2,1)S(1)} %fusion.39), channel_id=1, source_target_pairs={{16,8},{20,12},{24,16},{28,20},{17,9},{21,13},{25,17},{29,21},{18,... | collective-permute-start | bytes 786440 | tf_op jit(solution)/shard_map/ppermute | solution.py:355
  228.2 19.1 %collective-permute-start.37 = (bf16[256,512]{1,0:T(8,128)(2,1)S(1)}, bf16[256,512]{1,0:T(8,128)(2,1)S(1)}, u32[]{:S(2)}, u32[]{:S(2)}) collective-permute-start(bf16[256,512]{1,0:T(8,128)(2,1)S(1)} %fusion.37), channel_id=1, source_target_pairs={{0,8},{4,12},{8,16},{12,20},{1,9},{5,13},{9,17},{13,21},{2,10},{6,... | collective-permute-start | bytes 786440 | tf_op jit(solution)/shard_map/ppermute | solution.py:354
  233.7 15.2 %collective-permute-start.48 = (bf16[512,256]{1,0:T(8,128)(2,1)S(1)}, bf16[512,256]{1,0:T(8,128)(2,1)S(1)}, u32[]{:S(2)}, u32[]{:S(2)}) collective-permute-start(bf16[512,256]{1,0:T(8,128)(2,1)S(1)} %fusion.43), channel_id=1, source_target_pairs={{16,8},{20,12},{24,16},{28,20},{17,9},{21,13},{25,17},{29,21},{18,... | collective-permute-start | bytes 786440 | tf_op jit(solution)/shard_map/ppermute | solution.py:355
  234.7 19.2 %collective-permute-start.45 = (bf16[512,256]{1,0:T(8,128)(2,1)S(1)}, bf16[512,256]{1,0:T(8,128)(2,1)S(1)}, u32[]{:S(2)}, u32[]{:S(2)}) collective-permute-start(bf16[512,256]{1,0:T(8,128)(2,1)S(1)} %fusion.41), channel_id=1, source_target_pairs={{0,8},{4,12},{8,16},{12,20},{1,9},{5,13},{9,17},{13,21},{2,10},{6,... | collective-permute-start | bytes 786440 | tf_op jit(solution)/shard_map/ppermute | solution.py:354
  240.2 15.4 %collective-permute-start.27 = (bf16[256,512]{1,0:T(8,128)(2,1)S(1)}, bf16[256,512]{1,0:T(8,128)(2,1)S(1)}, u32[]{:S(2)}, u32[]{:S(2)}) collective-permute-start(bf16[256,512]{1,0:T(8,128)(2,1)S(1)} %fusion.30), channel_id=1, source_target_pairs={{8,0},{12,4},{16,8},{20,12},{24,16},{28,20},{9,1},{13,5},{17,9},{2... | collective-permute-start | bytes 786440 | tf_op jit(solution)/shard_map/ppermute | solution.py:355
  241.8 18.3 %collective-permute-start.24 = (bf16[256,512]{1,0:T(8,128)(2,1)S(1)}, bf16[256,512]{1,0:T(8,128)(2,1)S(1)}, u32[]{:S(2)}, u32[]{:S(2)}) collective-permute-start(bf16[256,512]{1,0:T(8,128)(2,1)S(1)} %fusion.28), channel_id=1, source_target_pairs={{0,8},{4,12},{8,16},{12,20},{16,24},{20,28},{1,9},{5,13},{9,17},{1... | collective-permute-start | bytes 786440 | tf_op jit(solution)/shard_map/ppermute | solution.py:354
  247.3 15.3 %collective-permute-start.34 = (bf16[256,512]{1,0:T(8,128)(2,1)S(1)}, bf16[256,512]{1,0:T(8,128)(2,1)S(1)}, u32[]{:S(2)}, u32[]{:S(2)}) collective-permute-start(bf16[256,512]{1,0:T(8,128)(2,1)S(1)} %fusion.34), channel_id=1, source_target_pairs={{8,0},{12,4},{16,8},{20,12},{24,16},{28,20},{9,1},{13,5},{17,9},{2... | collective-permute-start | bytes 786440 | tf_op jit(solution)/shard_map/ppermute | solution.py:355
  248.9 18.2 %collective-permute-start.31 = (bf16[256,512]{1,0:T(8,128)(2,1)S(1)}, bf16[256,512]{1,0:T(8,128)(2,1)S(1)}, u32[]{:S(2)}, u32[]{:S(2)}) collective-permute-start(bf16[256,512]{1,0:T(8,128)(2,1)S(1)} %fusion.32), channel_id=1, source_target_pairs={{0,8},{4,12},{8,16},{12,20},{16,24},{20,28},{1,9},{5,13},{9,17},{1... | collective-permute-start | bytes 786440 | tf_op jit(solution)/shard_map/ppermute | solution.py:354
  253.9 14.4 %collective-permute-start.41 = (bf16[256,512]{1,0:T(8,128)(2,1)S(1)}, bf16[256,512]{1,0:T(8,128)(2,1)S(1)}, u32[]{:S(2)}, u32[]{:S(2)}) collective-permute-start(bf16[256,512]{1,0:T(8,128)(2,1)S(1)} %fusion.38), channel_id=1, source_target_pairs={{8,0},{12,4},{16,8},{20,12},{24,16},{28,20},{9,1},{13,5},{17,9},{2... | collective-permute-start | bytes 786440 | tf_op jit(solution)/shard_map/ppermute | solution.py:355
  (46 other events, 264.6 us)
